TPU v7x, 32 devices: a whole 2x2x4 slice. The times are simulated.
32 devices in a mesh: grp: 2 (over x), row: 2 (over core), col: 8 (over z, y).
Axes of the slice: x: 2, y: 2, z: 4, core: 2. Of those that a mesh axis runs over, the one named last changes fastest.
Arguments:
- hidden_acts: bfloat16 [512, 26624], P(('grp', 'row'), 'col'), parts along dimension 0, may hold values from -216 to 216
- down_weight: bfloat16 [26624, 8192], P('col', 'row'), may hold values from -0.0390625 to 0.0390625
- amax_history: float32 [8], P('grp'), parts along dimension 0, may hold values from 3 to 12
Outputs:
- scaled_out: bfloat16 [512, 8192], P(('grp', 'col'), 'row'), parts along dimension 0
- token_scale: float32 [512], P(('grp', 'row')), parts along dimension 0
- history_next: float32 [8], P('grp'), parts along dimension 0
There are 2 independent parts, one for each index of `grp`. A program takes and returns all parts, laid end to end along the dimension named above; an argument that names none is the same for every part. Nothing has to cross between parts.
All inputs are finite; a program needn't handle non-finite values.
Results may differ from a plain program's by a relative error of at most 0.0044.
Values may be sent and summed in bfloat16 or wider, within the bound.
A program may use at most 64 MiB of HBM per device.

v0:
```python
import jax
import jax.numpy as jnp
from jax import lax
from jax.sharding import PartitionSpec as P

clip_ratio = 0.5
format_limit = 448.0


def clip_scaled(values, scales):
    return jnp.clip(
        values.astype(jnp.float32) / scales[:, None], -format_limit, format_limit
    ).astype(jnp.bfloat16)


def on_device(hidden_acts, down_weight, amax_history):
    local_peak = jnp.max(jnp.abs(hidden_acts), axis=1).astype(jnp.float32)
    token_peak = lax.pmax(local_peak, "col")
    own_scale = clip_ratio * (token_peak + 1e-06) / format_limit
    quantized = clip_scaled(hidden_acts, own_scale)
    all_quant = lax.all_gather(quantized, "row", axis=0, tiled=True)
    all_scale = lax.all_gather(own_scale, "row", axis=0, tiled=True)
    previous = jnp.max(amax_history)
    block_rows = all_quant.shape[0] // lax.axis_size("col")
    summed = lax.psum_scatter(
        jnp.dot(all_quant, down_weight, preferred_element_type=jnp.float32),
        "col",
        scatter_dimension=0,
        tiled=True,
    )
    block_scale = lax.dynamic_slice_in_dim(
        all_scale, lax.axis_index("col") * block_rows, block_rows
    )
    result = summed * block_scale[:, None]
    local_max = jnp.max(jnp.abs(result))
    scaled_out = jnp.clip(result / previous, -1.0, 1.0).astype(jnp.bfloat16)
    newest = lax.pmax(local_max, ("row", "col"))
    history_next = jnp.concatenate([newest[None], amax_history[:-1]])
    return (scaled_out, own_scale, history_next)


def solution(mesh):
    in_specs = (P(("grp", "row"), "col"), P("col", "row"), P("grp"))
    out_specs = (P(("grp", "col"), "row"), P(("grp", "row")), P("grp"))
    return jax.shard_map(
        on_device, mesh=mesh, in_specs=in_specs, out_specs=out_specs, check_vma=False
    )
```

profile of v0, /device:TPU:0, one launch (start us, length us, event | category | flops | bytes accessed | tf_op | source)
XLA Modules:
  0.0 189.1 jit_solution(5066335631180745152)
XLA Ops:
  7.2 0.0 all-gather.3.cloned.1.call-start
  7.2 1.4 abs_reduce_fusion
  8.6 23.1 %pmax.14 = f32[128]{0:T(128)S(1)} all-reduce(bf16[128]{0:T(256)(128)(2,1)S(1)} %abs_reduce_fusion), channel_id=1, replica_groups=mesh['grp'=2,'row'=2,'col'=8] {'col'}, use_global_device_ids=true, to_apply=%region_1.0 | all-reduce | flops 128 | bytes 768 | tf_op jit(solution)/shard_map/pmax | solution.py:18
  31.7 0.0 copy-start
  31.7 2.3 %clamp_convert_fusion = bf16[128,3328]{1,0:T(8,128)(2,1)} fusion(bf16[128,3328]{1,0:T(8,128)(2,1)} %param.3, f32[128]{0:T(128)S(1)} %add_multiply_fusion), kind=kLoop, calls=%fused_computation | loop fusion | flops 1703936 | bytes 1704448 | tf_op jit(solution)/shard_map/convert_element_type | solution.py:13
  34.1 0.0 all-gather.3.cloned.1.call-update
  34.1 0.0 reduce-scatter.2.cloned.1.call-start
  34.1 7.4 %all-gather.3.cloned.1.call-done = bf16[256,3328]{1,0:T(8,128)(2,1)} async-done(((bf16[128,3328]{1,0:T(8,128)(2,1)}), bf16[256,3328]{1,0:T(8,128)(2,1)}) %all-gather.3.cloned.1.call-update) | async-done | bytes 1703952 | tf_op jit(solution)/shard_map/all_gather | solution.py:21
  41.5 14.3 %fusion = f32[256,4096]{1,0:T(8,128)} fusion(bf16[256,3328]{1,0:T(8,128)(2,1)} %all-gather.3.cloned.1.call-done, bf16[3328,4096]{1,0:T(8,128)(2,1)} %param.4), kind=kOutput, calls=%fused_computation.6 | convolution fusion | flops 6979321856 | bytes 33161216 | tf_op jit(solution)/shard_map/dot_general | solution.py:26
  55.8 0.0 copy-done
  55.8 0.0 copy-start.1
  55.8 0.0 reduce-scatter.2.cloned.1.call-update
  55.8 1.8 all-gather
  57.6 0.1 dynamic_slice.3
  57.7 0.0 copy-done.1
  57.7 0.6 reduce_max.28
  58.3 86.8 %reduce-scatter.2.cloned.1.call-done = f32[32,4096]{1,0:T(8,128)} async-done(((f32[256,4096]{1,0:T(8,128)}), f32[32,4096]{1,0:T(8,128)}) %reduce-scatter.2.cloned.1.call-update) | async-done | bytes 524304 | tf_op jit(solution)/shard_map/reduce_scatter | solution.py:25
  145.1 3.2 %abs_reduce_fusion.1 = (f32[]{:T(128)}, bf16[32,4096]{1,0:T(8,128)(2,1)}) fusion(f32[32,4096]{1,0:T(8,128)} %reduce-scatter.2.cloned.1.call-done, f32[32]{0:T(128)S(1)} %dynamic_slice.3, f32[]{:T(128)} %reduce_max.28), kind=kLoop, calls=%fused_computation.2 | loop fusion | flops 786431 | bytes 786568 | tf_op jit(solution)/shard_map/reduce_max | solution.py:35
  148.3 32.9 %pmax.15 = f32[1]{0:T(128)} all-reduce(f32[1]{0:T(128)} %bitcast.2), channel_id=1, replica_groups=mesh['grp'=2,'row'=2,'col'=8] {'row','col'}, use_global_device_ids=true, to_apply=%region_5.6 | all-reduce | flops 1 | bytes 8 | tf_op jit(solution)/shard_map/pmax | solution.py:37
  181.2 1.1 pad_maximum_fusion
  (2 shorter events, 0.0 us)
Async XLA Ops:
  7.2 34.3 %all-gather.3.cloned.1.call-start = ((), (), s32[]{:S(2)}) async-start(), calls=%async_computation.1 | async-start | bytes 2555904 | tf_op jit(solution)/shard_map/all_gather | solution.py:21
  31.7 24.1 %copy-start = (f32[128]{0:T(128)}, f32[128]{0:T(128)S(1)}, u32[]{:S(2)}) copy-start(f32[128]{0:T(128)S(1)} %add_multiply_fusion) | copy-start | bytes 1540
  34.1 111.0 %reduce-scatter.2.cloned.1.call-start = ((), (), s32[]{:S(2)}) async-start(), calls=%async_computation.2 | async-start | bytes 4718592 | tf_op jit(solution)/shard_map/reduce_scatter | solution.py:25
  55.8 1.9 copy-start.1
Sparse Core Ops, SparseCore 0:
  34.2 7.2 all-gather.2
  55.9 89.0 reduce-scatter.1
where the time goes:
time: 189 us
  waiting for transfers between devices  94.2 us (50%)
  blocking collectives  57.8 us (31%)
  matrix products  14.3 us (8%)
  between operations  14.1 us (7%)
  other arithmetic  8.67 us (5%)
    reduce_scatter x1, waiting for transfers between devices, on_device(): lax.psum_scatter(jnp.dot(all_quant, down_weight, preferred_element_type=j...  86.8 us
    pmax x1, blocking collectives, on_device(): newest = lax.pmax(local_max, ('row', 'col'))  32.9 us
    pmax x1, blocking collectives, on_device(): token_peak = lax.pmax(local_peak, 'col')  23.1 us
    dot_general x1, matrix products, on_device(): jnp.dot(all_quant, down_weight, preferred_element_type=jnp.float32)  14.3 us
    all_gather x1, waiting for transfers between devices, on_device(): all_quant = lax.all_gather(quantized, 'row', axis=0, tiled=True)  7.36 us
  transfers between devices with their start and end apart: 2, of which 2 were waited for; matrix products, arithmetic and copies ran while one was open for 0% of the time, Pallas kernels for 0%

commit v1 on v0

v1 whole, which is shorter than its diff:
```python
import functools

import jax
import jax.numpy as jnp
from jax import lax
from jax.experimental import pallas as pl
from jax.experimental.pallas import tpu as pltpu
from jax.sharding import PartitionSpec as P

clip_ratio = 0.5
format_limit = 448.0
LANES = 128
CHUNK = 512
LAG = 2
MESH = pl.DeviceIdType.MESH
F32 = jnp.float32
BF16 = jnp.bfloat16


def kernel(
    n_row, n_col,
    h_ref, w_ref, hist_ref,
    out_ref, scale_ref, hist_out,
    hq, xq, lim, wv, pk, prec, ysend, yrecv, own, zsend, zrecv, mx, mrec,
    h_sem, hr_sem, w_sem, pk_send, pk_recv, y_sem, z_send, z_recv, m_send, m_recv,
):
    rows, depth = h_ref.shape
    groups = rows // LANES
    chunks = wv.shape[0]
    n_z = n_col // 2
    half = rows * n_row // 2
    block = rows * n_row // n_col
    peers = n_row * n_col
    r, c = lax.axis_index("row"), lax.axis_index("col")
    z, y = c // 2, lax.rem(c, 2)
    me = r * n_col + c
    my_rows = pl.ds(pl.multiple_of(r * rows, LANES), rows)

    def place(p):
        return {"row": p // n_col, "col": lax.rem(p, n_col)}

    def each_peer(do):
        def body(o, carry):
            do(o - 1, lax.rem(me + o, peers))
            return carry
        lax.fori_loop(1, peers, body, 0)

    barrier = pltpu.get_barrier_semaphore()
    each_peer(lambda i, p: pl.semaphore_signal(
        barrier, inc=1, device_id=place(p), device_id_type=MESH))

    own_copy = pltpu.make_async_copy(h_ref, hq.at[my_rows], h_sem)
    own_copy.start()

    def weight_copy(k):
        cols = pl.ds(pl.multiple_of(k * CHUNK, CHUNK), CHUNK)
        return pltpu.make_async_copy(w_ref.at[:, cols], wv.at[k], w_sem.at[k])

    for k in range(chunks):
        weight_copy(k).start()

    own_copy.wait()
    whole = depth // LANES
    for g in range(groups):
        at = pl.ds(pl.multiple_of(r * rows + g * LANES, LANES), LANES)
        m = jnp.abs(hq[at, 0:LANES])
        for j in range(1, whole):
            m = jnp.maximum(m, jnp.abs(hq[at, j * LANES:(j + 1) * LANES]))
        m = m.astype(F32)
        if depth % LANES:
            tail = jnp.abs(hq[at, whole * LANES:].astype(F32))
            m = jnp.maximum(m, jnp.max(tail, axis=1, keepdims=True))
        peak = jnp.max(jnp.transpose(m), axis=0, keepdims=True)
        pk[g:g + 1, :] = peak
        prec[me, g:g + 1, :] = peak

    pl.semaphore_wait(barrier, peers - 1)

    def peak_copy(i, p, slot):
        return pltpu.make_async_remote_copy(
            src_ref=pk, dst_ref=prec.at[slot], send_sem=pk_send.at[i],
            recv_sem=pk_recv.at[slot], device_id=place(p), device_id_type=MESH)

    each_peer(lambda i, p: peak_copy(i, p, me).start())
    acts_copies = []
    for o in range(1, n_row):
        to = lax.rem(r + o, n_row)
        acts_copies.append(pltpu.make_async_remote_copy(
            src_ref=hq.at[my_rows], dst_ref=hq.at[my_rows], send_sem=hr_sem.at[0, o - 1],
            recv_sem=hr_sem.at[1, o - 1], device_id={"row": to}, device_id_type=MESH))
    for copy in acts_copies:
        copy.start()

    each_peer(lambda i, p: peak_copy(i, p, p).wait_recv())
    for q in range(n_row):
        top = jnp.max(prec[q * n_col:(q + 1) * n_col], axis=0)
        for g in range(groups):
            edge = clip_ratio * (top[g:g + 1] + 1e-06)
            wide = jnp.transpose(jnp.broadcast_to(edge, (LANES, LANES)))
            at = q * rows + g * LANES
            lim[at:at + LANES, :] = wide.astype(BF16)
    mine = jnp.max(prec[pl.ds(r * n_col, n_col)], axis=0)
    scale_ref[...] = clip_ratio * (mine + 1e-06) / format_limit

    for copy in acts_copies:
        copy.wait_recv()

    def clip_block(b, carry):
        zt, side = b // 2, lax.rem(b, 2)
        col_at = 2 * zt + jnp.where(side == 0, 1 - y, y)
        src = pl.ds(pl.multiple_of(col_at * block, block), block)
        dst = pl.ds(pl.multiple_of(side * half + zt * block, block), block)
        edge = lim[src, :]
        for j in range(pl.cdiv(depth, LANES)):
            lo, hi = j * LANES, min((j + 1) * LANES, depth)
            e = edge[:, :hi - lo]
            xq[dst, lo:hi] = jnp.minimum(jnp.maximum(hq[src, lo:hi], -e), e)
        return carry

    lax.fori_loop(0, n_col, clip_block, 0)

    previous = hist_ref[0]
    for i in range(1, hist_ref.shape[0]):
        previous = jnp.maximum(previous, hist_ref[i])
    mx[...] = jnp.zeros_like(mx)

    def y_copy(k):
        return pltpu.make_async_remote_copy(
            src_ref=ysend.at[k], dst_ref=yrecv.at[k], send_sem=y_sem.at[0, k],
            recv_sem=y_sem.at[1, k], device_id={"col": 2 * z + 1 - y}, device_id_type=MESH)

    def z_copy(k, d):
        zt = lax.rem(z + d, n_z)
        src = pl.ds(pl.multiple_of(zt * block, block), block)
        return pltpu.make_async_remote_copy(
            src_ref=zsend.at[k, src], dst_ref=zrecv.at[k, d - 1], send_sem=z_send.at[k, d - 1],
            recv_sem=z_recv.at[k, d - 1], device_id={"col": 2 * zt + y}, device_id_type=MESH)

    def multiply(k):
        weight_copy(k).wait()
        p = jnp.dot(xq[...], wv[k], preferred_element_type=F32)
        ysend[k] = p[:half].astype(BF16)
        own[k] = p[half:]
        y_copy(k).start()

    def add_y(k):
        y_copy(k).wait_recv()
        s = own[k] + yrecv[k].astype(F32)
        own[k] = s
        zsend[k] = s.astype(BF16)
        for d in range(1, n_z):
            z_copy(k, d).start()

    def add_z(k):
        s = own[k, pl.ds(pl.multiple_of(z * block, block), block)]
        for d in range(1, n_z):
            z_copy(k, d).wait_recv()
            s = s + zrecv[k, d - 1].astype(F32)
        m = jnp.max(jnp.abs(s), axis=0, keepdims=True)
        for j in range(CHUNK // LANES):
            mx[...] = jnp.maximum(mx[...], m[:, j * LANES:(j + 1) * LANES])
        cols = pl.ds(pl.multiple_of(k * CHUNK, CHUNK), CHUNK)
        out_ref[:, cols] = jnp.clip(s / previous, -1.0, 1.0).astype(BF16)

    def step(k, carry):
        pl.when(k < chunks)(lambda: multiply(k))
        pl.when(jnp.logical_and(k >= LAG, k < chunks + LAG))(lambda: add_y(k - LAG))
        pl.when(k >= 2 * LAG)(lambda: add_z(k - 2 * LAG))
        return carry

    lax.fori_loop(0, chunks + 2 * LAG, step, 0)

    mrec[me] = mx[...]

    def max_copy(i, p, slot):
        return pltpu.make_async_remote_copy(
            src_ref=mx, dst_ref=mrec.at[slot], send_sem=m_send.at[i],
            recv_sem=m_recv.at[slot], device_id=place(p), device_id_type=MESH)

    each_peer(lambda i, p: max_copy(i, p, me).start())

    def sent(k, carry):
        y_copy(k).wait_send()
        for d in range(1, n_z):
            z_copy(k, d).wait_send()
        return carry

    lax.fori_loop(0, chunks, sent, 0)
    each_peer(lambda i, p: peak_copy(i, p, me).wait_send())
    for copy in acts_copies:
        copy.wait_send()
    each_peer(lambda i, p: max_copy(i, p, p).wait_recv())
    hist_out[0] = jnp.max(mrec[...])
    for i in range(1, hist_ref.shape[0]):
        hist_out[i] = hist_ref[i - 1]
    each_peer(lambda i, p: max_copy(i, p, me).wait_send())


def on_device(n_row, n_col, hidden_acts, down_weight, amax_history):
    rows, depth = hidden_acts.shape
    width = down_weight.shape[1]
    groups = rows // LANES
    tokens = rows * n_row
    half, block, chunks, n_z = tokens // 2, tokens // n_col, width // CHUNK, n_col // 2
    peers = n_row * n_col
    dma = pltpu.SemaphoreType.DMA
    vmem = pl.BlockSpec(memory_space=pltpu.VMEM)
    smem = pl.BlockSpec(memory_space=pltpu.SMEM)
    anywhere = pl.BlockSpec(memory_space=pl.ANY)
    scaled_out, scale, history = pl.pallas_call(
        functools.partial(kernel, n_row, n_col),
        out_shape=(
            jax.ShapeDtypeStruct((block, width), BF16),
            jax.ShapeDtypeStruct((groups, LANES), F32),
            jax.ShapeDtypeStruct(amax_history.shape, F32),
        ),
        in_specs=[anywhere, anywhere, smem],
        out_specs=(vmem, vmem, smem),
        scratch_shapes=[
            pltpu.VMEM((tokens, depth), BF16),
            pltpu.VMEM((tokens, depth), BF16),
            pltpu.VMEM((tokens, LANES), BF16),
            pltpu.VMEM((chunks, depth, CHUNK), BF16),
            pltpu.VMEM((groups, LANES), F32),
            pltpu.VMEM((peers, groups, LANES), F32),
            pltpu.VMEM((chunks, half, CHUNK), BF16),
            pltpu.VMEM((chunks, half, CHUNK), BF16),
            pltpu.VMEM((chunks, half, CHUNK), F32),
            pltpu.VMEM((chunks, half, CHUNK), BF16),
            pltpu.VMEM((chunks, n_z - 1, block, CHUNK), BF16),
            pltpu.VMEM((1, LANES), F32),
            pltpu.VMEM((peers, 1, LANES), F32),
            dma, dma((2, n_row - 1)), dma((chunks,)), dma((peers,)), dma((peers,)),
            dma((2, chunks)), dma((chunks, n_z - 1)), dma((chunks, n_z - 1)),
            dma((peers,)), dma((peers,)),
        ],
        compiler_params=pltpu.CompilerParams(
            collective_id=0, has_side_effects=True, vmem_limit_bytes=56 << 20),
        cost_estimate=pl.CostEstimate(
            flops=2 * tokens * depth * width, bytes_accessed=2 * depth * width, transcendentals=0),
    )(hidden_acts, down_weight, amax_history)
    return scaled_out, scale.reshape(rows), history


def solution(mesh):
    in_specs = (P(("grp", "row"), "col"), P("col", "row"), P("grp"))
    out_specs = (P(("grp", "col"), "row"), P(("grp", "row")), P("grp"))
    return jax.shard_map(
        functools.partial(on_device, mesh.shape["row"], mesh.shape["col"]),
        mesh=mesh, in_specs=in_specs, out_specs=out_specs, check_vma=False)
```

time: 189 us -> 58.9 us (0.31)
  waiting for transfers between devices: 94.2 us -> 0 us
  blocking collectives: 57.8 us -> 0 us
  Pallas kernels: 0 us -> 54.2 us
  matrix products: 14.3 us -> 0 us
  between operations: 14.1 us -> 0.64 us
  other arithmetic: 8.67 us -> 0 us
  local copies, waits for them, and re-layouts: 0.08 us -> 3.88 us
    reduce_scatter x1 -> x0, waiting for transfers between devices: 86.8 us -> none  [on_device(): lax.psum_scatter(jnp.dot(all_quant, down_weight, preferred_element_type=j...]
    pmax x2 -> x0, blocking collectives: 56 us -> none  [the longest x1 32.9 us: on_device(): newest = lax.pmax(local_max, ('row', 'col'))]
    pallas_call x0 -> x1, Pallas kernels: none -> 54.2 us  [on_device(): pl.pallas_call(functools.partial(kernel, n_row, n_col), out_shape=(jax.Sh...]
    dot_general x1 -> x0, matrix products: 14.3 us -> none  [on_device(): jnp.dot(all_quant, down_weight, preferred_element_type=jnp.float32)]
    all_gather x1 -> x0, waiting for transfers between devices: 7.36 us -> none  [on_device(): all_quant = lax.all_gather(quantized, 'row', axis=0, tiled=True)]
    reduce_max x3 -> x0, other arithmetic: 5.19 us -> none  [the longest x1 3.2 us: on_device(): local_max = jnp.max(jnp.abs(result))]
    unnamed x4 -> x3, local copies, waits for them, and re-layouts: 0.01 us -> 3.88 us
    convert_element_type x1 -> x0, other arithmetic: 2.33 us -> none  [clip_scaled(): return jnp.clip(values.astype(jnp.float32) / scales[:, None], -format_lim...]
  transfers between devices with their start and end apart: 2 -> 0, of which waited for: 2 -> 0; matrix products, arithmetic and copies ran while one was open for 0% -> 0% of each run, Pallas kernels for 0% -> 0%
where the time goes in v1:
time: 58.9 us; the launch traced here: 58.7 us
  Pallas kernels  54.2 us (92%)
  local copies, waits for them, and re-layouts  3.88 us (7%)
  between operations  0.64 us (1%)
    pallas_call x1, Pallas kernels, on_device(): pl.pallas_call(functools.partial(kernel, n_row, n_col), out_shape=(jax.Sh...  54.2 us
    unnamed x3, local copies, waits for them, and re-layouts  3.88 us

profile of v1, /device:TPU:0, one launch (start us, length us, event | category | flops | bytes accessed | tf_op | source)
XLA Modules:
  0.0 58.7 jit_solution(15366744924387708679)
XLA Ops:
  0.6 54.2 %shard_map.58 = (bf16[32,4096]{1,0:T(8,128)(2,1)}, f32[1,128]{1,0:T(1,128)}, f32[4]{0:T(128)}) custom-call(bf16[128,3328]{1,0:T(8,128)(2,1)} %h_ref.1, bf16[3328,4096]{1,0:T(8,128)(2,1)} %w_ref.1, f32[4]{0:T(128)} %hist_ref.1), custom_call_target="tpu_custom_call" | custom-call | flops 6979321856 | bytes 27262976 | tf_op jit(solution)/shard_map/pallas_call | solution.py:210
  54.8 1.7 %copy.9 = bf16[32,4096]{1,0:T(8,128)(2,1)} copy(bf16[32,4096]{1,0:T(8,128)(2,1)} %get-tuple-element.12) | data formatting | bytes 524288
  56.5 1.1 %copy.10 = f32[128]{0:T(128)} copy(f32[128]{0:T(128)} %bitcast.1) | data formatting | bytes 1024
  57.6 1.1 %copy.11 = f32[4]{0:T(128)} copy(f32[4]{0:T(128)} %get-tuple-element.14) | data formatting | bytes 32

commit v2 on v1

--- a/solution.py
+++ b/solution.py
@@ -10,8 +10,9 @@
 clip_ratio = 0.5
 format_limit = 448.0
 LANES = 128
-CHUNK = 512
-LAG = 2
+CHUNK = 256
+LAG = 3
+EARLY = 4
 MESH = pl.DeviceIdType.MESH
 F32 = jnp.float32
 BF16 = jnp.bfloat16
@@ -56,7 +57,7 @@
         cols = pl.ds(pl.multiple_of(k * CHUNK, CHUNK), CHUNK)
         return pltpu.make_async_copy(w_ref.at[:, cols], wv.at[k], w_sem.at[k])
 
-    for k in range(chunks):
+    for k in range(EARLY):
         weight_copy(k).start()
 
     own_copy.wait()
@@ -90,6 +91,8 @@
             recv_sem=hr_sem.at[1, o - 1], device_id={"row": to}, device_id_type=MESH))
     for copy in acts_copies:
         copy.start()
+    for k in range(EARLY, chunks):
+        weight_copy(k).start()
 
     each_peer(lambda i, p: peak_copy(i, p, p).wait_recv())
     for q in range(n_row):
@@ -196,6 +199,13 @@
     each_peer(lambda i, p: max_copy(i, p, me).wait_send())
 
 
+def write_out(a_ref, b_ref, c_ref, a_out, b_out, c_out):
+    a_out[...] = a_ref[...]
+    b_out[...] = b_ref[...]
+    for i in range(c_ref.shape[0]):
+        c_out[i] = c_ref[i]
+
+
 def on_device(n_row, n_col, hidden_acts, down_weight, amax_history):
     rows, depth = hidden_acts.shape
     width = down_weight.shape[1]
@@ -207,13 +217,14 @@
     vmem = pl.BlockSpec(memory_space=pltpu.VMEM)
     smem = pl.BlockSpec(memory_space=pltpu.SMEM)
     anywhere = pl.BlockSpec(memory_space=pl.ANY)
-    scaled_out, scale, history = pl.pallas_call(
+    out_shape = (
+        jax.ShapeDtypeStruct((block, width), BF16),
+        jax.ShapeDtypeStruct((groups, LANES), F32),
+        jax.ShapeDtypeStruct(amax_history.shape, F32),
+    )
+    results = pl.pallas_call(
         functools.partial(kernel, n_row, n_col),
-        out_shape=(
-            jax.ShapeDtypeStruct((block, width), BF16),
-            jax.ShapeDtypeStruct((groups, LANES), F32),
-            jax.ShapeDtypeStruct(amax_history.shape, F32),
-        ),
+        out_shape=out_shape,
         in_specs=[anywhere, anywhere, smem],
         out_specs=(vmem, vmem, smem),
         scratch_shapes=[
@@ -239,6 +250,10 @@
         cost_estimate=pl.CostEstimate(
             flops=2 * tokens * depth * width, bytes_accessed=2 * depth * width, transcendentals=0),
     )(hidden_acts, down_weight, amax_history)
+    scaled_out, scale, history = pl.pallas_call(
+        write_out, out_shape=out_shape, in_specs=[vmem, vmem, smem], out_specs=(vmem, vmem, smem),
+        compiler_params=pltpu.CompilerParams(vmem_limit_bytes=60 << 20),
+    )(*results)
     return scaled_out, scale.reshape(rows), history
 
 

time: 58.9 us -> 50.4 us (0.86)
  Pallas kernels: 54.2 us -> 49.6 us
  local copies, waits for them, and re-layouts: 3.88 us -> 0 us
    pallas_call x1 -> x2, Pallas kernels: 54.2 us -> 49.6 us  [the longest x1 47.9 us: on_device(): pl.pallas_call(functools.partial(kernel, n_row, n_col), out_shape=out_sha...]
    unnamed x3 -> x0, local copies, waits for them, and re-layouts: 3.88 us -> none
where the time goes in v2:
time: 50.4 us; the launch traced here: 50.3 us
  Pallas kernels  49.6 us (98%)
  between operations  0.64 us (1%)
    pallas_call x1, Pallas kernels, on_device(): pl.pallas_call(functools.partial(kernel, n_row, n_col), out_shape=out_sha...  47.9 us
    pallas_call x1, Pallas kernels, on_device(): pl.pallas_call(write_out, out_shape=out_shape, in_specs=[vmem, vmem, smem...  1.7 us

profile of v2, /device:TPU:0, one launch (start us, length us, event | category | flops | bytes accessed | tf_op | source)
XLA Modules:
  0.0 50.3 jit_solution(9128217847483098129)
XLA Ops:
  0.6 47.9 %shard_map.58 = (bf16[32,4096]{1,0:T(8,128)(2,1)}, f32[1,128]{1,0:T(1,128)}, f32[4]{0:T(128)}) custom-call(bf16[128,3328]{1,0:T(8,128)(2,1)} %h_ref.1, bf16[3328,4096]{1,0:T(8,128)(2,1)} %w_ref.1, f32[4]{0:T(128)} %hist_ref.1), custom_call_target="tpu_custom_call" | custom-call | flops 6979321856 | bytes 27262976 | tf_op jit(solution)/shard_map/pallas_call | solution.py:225
  48.6 1.7 %shard_map.59 = (bf16[32,4096]{1,0:T(8,128)(2,1)}, f32[1,128]{1,0:T(1,128)}, f32[4]{0:T(128)}) custom-call(bf16[32,4096]{1,0:T(8,128)(2,1)} %get-tuple-element.9.a_ref, f32[1,128]{1,0:T(1,128)} %get-tuple-element.10.b_ref, f32[4]{0:T(128)} %get-tuple-element.11.c_ref), custom_call_target="tpu_custom_call" | custom-call | tf_op jit(solution)/shard_map/pallas_call | solution.py:253

commit v3 on v2

--- a/solution.py
+++ b/solution.py
@@ -22,18 +22,19 @@
     n_row, n_col,
     h_ref, w_ref, hist_ref,
     out_ref, scale_ref, hist_out,
-    hq, xq, lim, wv, pk, prec, ysend, yrecv, own, zsend, zrecv, mx, mrec,
-    h_sem, hr_sem, w_sem, pk_send, pk_recv, y_sem, z_send, z_recv, m_send, m_recv,
+    hq, xq, lim, wv, pk, prec, send1, recv1, own, send2, recv2, send3, recv3, mx, mrec,
+    h_sem, hr_sem, w_sem, pk_send, pk_recv, s1_sem, s2_sem, s3_send, s3_recv, m_send, m_recv,
 ):
     rows, depth = h_ref.shape
     groups = rows // LANES
     chunks = wv.shape[0]
-    n_z = n_col // 2
+    n_far = n_col // 4
     half = rows * n_row // 2
+    quarter = half // 2
     block = rows * n_row // n_col
     peers = n_row * n_col
     r, c = lax.axis_index("row"), lax.axis_index("col")
-    z, y = c // 2, lax.rem(c, 2)
+    far, near, y = c // 4, lax.rem(c // 2, 2), lax.rem(c, 2)
     me = r * n_col + c
     my_rows = pl.ds(pl.multiple_of(r * rows, LANES), rows)
 
@@ -109,10 +110,12 @@
         copy.wait_recv()
 
     def clip_block(b, carry):
-        zt, side = b // 2, lax.rem(b, 2)
-        col_at = 2 * zt + jnp.where(side == 0, 1 - y, y)
+        part, d = b // n_far, lax.rem(b, n_far)
+        to_y = lax.rem(y + 1 - part // 2, 2)
+        to_near = lax.rem(near + 1 - lax.rem(part, 2), 2)
+        col_at = 4 * lax.rem(far + d, n_far) + 2 * to_near + to_y
         src = pl.ds(pl.multiple_of(col_at * block, block), block)
-        dst = pl.ds(pl.multiple_of(side * half + zt * block, block), block)
+        dst = pl.ds(pl.multiple_of(b * block, block), block)
         edge = lim[src, :]
         for j in range(pl.cdiv(depth, LANES)):
             lo, hi = j * LANES, min((j + 1) * LANES, depth)
@@ -127,38 +130,61 @@
         previous = jnp.maximum(previous, hist_ref[i])
     mx[...] = jnp.zeros_like(mx)
 
-    def y_copy(k):
-        return pltpu.make_async_remote_copy(
-            src_ref=ysend.at[k], dst_ref=yrecv.at[k], send_sem=y_sem.at[0, k],
-            recv_sem=y_sem.at[1, k], device_id={"col": 2 * z + 1 - y}, device_id_type=MESH)
-
-    def z_copy(k, d):
-        zt = lax.rem(z + d, n_z)
-        src = pl.ds(pl.multiple_of(zt * block, block), block)
-        return pltpu.make_async_remote_copy(
-            src_ref=zsend.at[k, src], dst_ref=zrecv.at[k, d - 1], send_sem=z_send.at[k, d - 1],
-            recv_sem=z_recv.at[k, d - 1], device_id={"col": 2 * zt + y}, device_id_type=MESH)
+    y_peer = 4 * far + 2 * near + 1 - y
+    near_peer = 4 * far + 2 * (1 - near) + y
+
+    def near_first(k):
+        return lax.rem(k, 4) == 1
+
+    def copy1(k):
+        return pltpu.make_async_remote_copy(
+            src_ref=send1.at[k], dst_ref=recv1.at[k], send_sem=s1_sem.at[0, k],
+            recv_sem=s1_sem.at[1, k], device_id_type=MESH,
+            device_id={"col": jnp.where(near_first(k), near_peer, y_peer)})
+
+    def copy2(k):
+        return pltpu.make_async_remote_copy(
+            src_ref=send2.at[k], dst_ref=recv2.at[k], send_sem=s2_sem.at[0, k],
+            recv_sem=s2_sem.at[1, k], device_id_type=MESH,
+            device_id={"col": jnp.where(near_first(k), y_peer, near_peer)})
+
+    def copy3(k, d):
+        to = 4 * lax.rem(far + d, n_far) + 2 * near + y
+        return pltpu.make_async_remote_copy(
+            src_ref=send3.at[k, d - 1], dst_ref=recv3.at[k, d - 1],
+            send_sem=s3_send.at[k, d - 1], recv_sem=s3_recv.at[k, d - 1],
+            device_id={"col": to}, device_id_type=MESH)
 
     def multiply(k):
         weight_copy(k).wait()
         p = jnp.dot(xq[...], wv[k], preferred_element_type=F32)
-        ysend[k] = p[:half].astype(BF16)
-        own[k] = p[half:]
-        y_copy(k).start()
-
-    def add_y(k):
-        y_copy(k).wait_recv()
-        s = own[k] + yrecv[k].astype(F32)
-        own[k] = s
-        zsend[k] = s.astype(BF16)
-        for d in range(1, n_z):
-            z_copy(k, d).start()
-
-    def add_z(k):
-        s = own[k, pl.ds(pl.multiple_of(z * block, block), block)]
-        for d in range(1, n_z):
-            z_copy(k, d).wait_recv()
-            s = s + zrecv[k, d - 1].astype(F32)
+        p1, p2 = p[quarter:half], p[half:half + quarter]
+        swap = near_first(k)
+        send1[k, :quarter] = p[:quarter].astype(BF16)
+        send1[k, quarter:] = jnp.where(swap, p2, p1).astype(BF16)
+        copy1(k).start()
+        own[k, :quarter] = jnp.where(swap, p1, p2)
+        own[k, quarter:] = p[half + quarter:]
+
+    def add1(k):
+        copy1(k).wait_recv()
+        send2[k] = (own[k, :quarter] + recv1[k, :quarter].astype(F32)).astype(BF16)
+        copy2(k).start()
+        own[k, quarter:] = own[k, quarter:] + recv1[k, quarter:].astype(F32)
+
+    def add2(k):
+        copy2(k).wait_recv()
+        s = own[k, quarter:] + recv2[k].astype(F32)
+        for d in range(1, n_far):
+            send3[k, d - 1] = s[d * block:(d + 1) * block].astype(BF16)
+            copy3(k, d).start()
+        own[k, :block] = s[:block]
+
+    def add3(k):
+        s = own[k, :block]
+        for d in range(1, n_far):
+            copy3(k, d).wait_recv()
+            s = s + recv3[k, d - 1].astype(F32)
         m = jnp.max(jnp.abs(s), axis=0, keepdims=True)
         for j in range(CHUNK // LANES):
             mx[...] = jnp.maximum(mx[...], m[:, j * LANES:(j + 1) * LANES])
@@ -166,12 +192,15 @@
         out_ref[:, cols] = jnp.clip(s / previous, -1.0, 1.0).astype(BF16)
 
     def step(k, carry):
-        pl.when(k < chunks)(lambda: multiply(k))
-        pl.when(jnp.logical_and(k >= LAG, k < chunks + LAG))(lambda: add_y(k - LAG))
-        pl.when(k >= 2 * LAG)(lambda: add_z(k - 2 * LAG))
+        def at(lag, do):
+            pl.when(jnp.logical_and(k >= lag, k < chunks + lag))(lambda: do(k - lag))
+        at(0, multiply)
+        at(LAG, add1)
+        at(2 * LAG, add2)
+        at(3 * LAG, add3)
         return carry
 
-    lax.fori_loop(0, chunks + 2 * LAG, step, 0)
+    lax.fori_loop(0, chunks + 3 * LAG, step, 0)
 
     mrec[me] = mx[...]
 
@@ -183,9 +212,10 @@
     each_peer(lambda i, p: max_copy(i, p, me).start())
 
     def sent(k, carry):
-        y_copy(k).wait_send()
-        for d in range(1, n_z):
-            z_copy(k, d).wait_send()
+        copy1(k).wait_send()
+        copy2(k).wait_send()
+        for d in range(1, n_far):
+            copy3(k, d).wait_send()
         return carry
 
     lax.fori_loop(0, chunks, sent, 0)
@@ -211,7 +241,7 @@
     width = down_weight.shape[1]
     groups = rows // LANES
     tokens = rows * n_row
-    half, block, chunks, n_z = tokens // 2, tokens // n_col, width // CHUNK, n_col // 2
+    half, block, chunks, n_far = tokens // 2, tokens // n_col, width // CHUNK, n_col // 4
     peers = n_row * n_col
     dma = pltpu.SemaphoreType.DMA
     vmem = pl.BlockSpec(memory_space=pltpu.VMEM)
@@ -237,12 +267,14 @@
             pltpu.VMEM((chunks, half, CHUNK), BF16),
             pltpu.VMEM((chunks, half, CHUNK), BF16),
             pltpu.VMEM((chunks, half, CHUNK), F32),
-            pltpu.VMEM((chunks, half, CHUNK), BF16),
-            pltpu.VMEM((chunks, n_z - 1, block, CHUNK), BF16),
+            pltpu.VMEM((chunks, half // 2, CHUNK), BF16),
+            pltpu.VMEM((chunks, half // 2, CHUNK), BF16),
+            pltpu.VMEM((chunks, n_far - 1, block, CHUNK), BF16),
+            pltpu.VMEM((chunks, n_far - 1, block, CHUNK), BF16),
             pltpu.VMEM((1, LANES), F32),
             pltpu.VMEM((peers, 1, LANES), F32),
             dma, dma((2, n_row - 1)), dma((chunks,)), dma((peers,)), dma((peers,)),
-            dma((2, chunks)), dma((chunks, n_z - 1)), dma((chunks, n_z - 1)),
+            dma((2, chunks)), dma((2, chunks)), dma((chunks, n_far - 1)), dma((chunks, n_far - 1)),
             dma((peers,)), dma((peers,)),
         ],
         compiler_params=pltpu.CompilerParams(

time: 50.4 us -> 49.8 us (0.988)
  Pallas kernels: 49.6 us -> 49 us
    pallas_call x1, Pallas kernels: 47.9 us -> 47.3 us  [on_device(): pl.pallas_call(functools.partial(kernel, n_row, n_col), out_shape=out_sha...]
where the time goes in v3:
time: 49.8 us; the launch traced here: 49.7 us
  Pallas kernels  49 us (98%)
  between operations  0.64 us (1%)
    pallas_call x1, Pallas kernels, on_device(): pl.pallas_call(functools.partial(kernel, n_row, n_col), out_shape=out_sha...  47.3 us
    pallas_call x1, Pallas kernels, on_device(): pl.pallas_call(write_out, out_shape=out_shape, in_specs=[vmem, vmem, smem...  1.7 us

profile of v3, /device:TPU:0, one launch (start us, length us, event | category | flops | bytes accessed | tf_op | source)
XLA Modules:
  0.0 49.7 jit_solution(6177199139249145726)
XLA Ops:
  0.6 47.3 %shard_map.58 = (bf16[32,4096]{1,0:T(8,128)(2,1)}, f32[1,128]{1,0:T(1,128)}, f32[4]{0:T(128)}) custom-call(bf16[128,3328]{1,0:T(8,128)(2,1)} %h_ref.1, bf16[3328,4096]{1,0:T(8,128)(2,1)} %w_ref.1, f32[4]{0:T(128)} %hist_ref.1), custom_call_target="tpu_custom_call" | custom-call | flops 6979321856 | bytes 27262976 | tf_op jit(solution)/shard_map/pallas_call | solution.py:255
  48.0 1.7 %shard_map.59 = (bf16[32,4096]{1,0:T(8,128)(2,1)}, f32[1,128]{1,0:T(1,128)}, f32[4]{0:T(128)}) custom-call(bf16[32,4096]{1,0:T(8,128)(2,1)} %get-tuple-element.9.a_ref, f32[1,128]{1,0:T(1,128)} %get-tuple-element.10.b_ref, f32[4]{0:T(128)} %get-tuple-element.11.c_ref), custom_call_target="tpu_custom_call" | custom-call | tf_op jit(solution)/shard_map/pallas_call | solution.py:285

commit v4 on v3

--- a/solution.py
+++ b/solution.py
@@ -133,6 +133,8 @@
     y_peer = 4 * far + 2 * near + 1 - y
     near_peer = 4 * far + 2 * (1 - near) + y
 
+    cut = (depth // 256 + 1) // 2 * 256
+
     def near_first(k):
         return lax.rem(k, 4) == 1
 
@@ -157,7 +159,9 @@
 
     def multiply(k):
         weight_copy(k).wait()
-        p = jnp.dot(xq[...], wv[k], preferred_element_type=F32)
+        pa = jnp.dot(xq[:, :cut], wv[k, :cut], preferred_element_type=F32)
+        pb = jnp.dot(xq[:, cut:], wv[k, cut:], preferred_element_type=F32)
+        p = pa + pb
         p1, p2 = p[quarter:half], p[half:half + quarter]
         swap = near_first(k)
         send1[k, :quarter] = p[:quarter].astype(BF16)
@@ -229,11 +233,13 @@
     each_peer(lambda i, p: max_copy(i, p, me).wait_send())
 
 
-def write_out(a_ref, b_ref, c_ref, a_out, b_out, c_out):
-    a_out[...] = a_ref[...]
-    b_out[...] = b_ref[...]
-    for i in range(c_ref.shape[0]):
-        c_out[i] = c_ref[i]
+def write_out(a_ref, b_ref, c_ref, a_out, b_out, c_out, sems):
+    pairs = ((a_ref, a_out), (b_ref, b_out), (c_ref, c_out))
+    copies = [pltpu.make_async_copy(a, b, sems.at[i]) for i, (a, b) in enumerate(pairs)]
+    for copy in copies:
+        copy.start()
+    for copy in copies:
+        copy.wait()
 
 
 def on_device(n_row, n_col, hidden_acts, down_weight, amax_history):
@@ -283,7 +289,8 @@
             flops=2 * tokens * depth * width, bytes_accessed=2 * depth * width, transcendentals=0),
     )(hidden_acts, down_weight, amax_history)
     scaled_out, scale, history = pl.pallas_call(
-        write_out, out_shape=out_shape, in_specs=[vmem, vmem, smem], out_specs=(vmem, vmem, smem),
+        write_out, out_shape=out_shape, in_specs=[anywhere] * 3, out_specs=(anywhere,) * 3,
+        scratch_shapes=[dma((3,))],
         compiler_params=pltpu.CompilerParams(vmem_limit_bytes=60 << 20),
     )(*results)
     return scaled_out, scale.reshape(rows), history

time: 49.8 us -> 57.2 us (1.15)
  Pallas kernels: 49 us -> 56.4 us
    pallas_call x1, Pallas kernels: 1.7 us -> 9.1 us  [on_device(): pl.pallas_call(write_out, out_shape=out_shape, in_specs=[anywhere] * 3, o...]
where the time goes in v4:
time: 57.2 us; the launch traced here: 57.1 us
  Pallas kernels  56.4 us (99%)
  between operations  0.64 us (1%)
    pallas_call x1, Pallas kernels, on_device(): pl.pallas_call(functools.partial(kernel, n_row, n_col), out_shape=out_sha...  47.3 us
    pallas_call x1, Pallas kernels, on_device(): pl.pallas_call(write_out, out_shape=out_shape, in_specs=[anywhere] * 3, o...  9.1 us

profile of v4, /device:TPU:0, one launch (start us, length us, event | category | flops | bytes accessed | tf_op | source)
XLA Modules:
  0.0 57.1 jit_solution(1140670048769979641)
XLA Ops:
  0.6 47.3 %shard_map.58 = (bf16[32,4096]{1,0:T(8,128)(2,1)}, f32[1,128]{1,0:T(1,128)}, f32[4]{0:T(128)}) custom-call(bf16[128,3328]{1,0:T(8,128)(2,1)} %h_ref.1, bf16[3328,4096]{1,0:T(8,128)(2,1)} %w_ref.1, f32[4]{0:T(128)} %hist_ref.1), custom_call_target="tpu_custom_call" | custom-call | flops 6979321856 | bytes 27262976 | tf_op jit(solution)/shard_map/pallas_call | solution.py:261
  48.0 9.1 %shard_map.59 = (bf16[32,4096]{1,0:T(8,128)(2,1)}, f32[1,128]{1,0:T(1,128)}, f32[4]{0:T(128)}) custom-call(bf16[32,4096]{1,0:T(8,128)(2,1)} %get-tuple-element.9.a_ref, f32[1,128]{1,0:T(1,128)} %get-tuple-element.10.b_ref, f32[4]{0:T(128)} %get-tuple-element.11.c_ref), custom_call_target="tpu_custom_call" | custom-call | tf_op jit(solution)/shard_map/pallas_call | solution.py:291

commit v5 on v3

--- a/solution.py
+++ b/solution.py
@@ -11,7 +11,7 @@
 format_limit = 448.0
 LANES = 128
 CHUNK = 256
-LAG = 3
+LAGS = (5, 8, 11)
 EARLY = 4
 MESH = pl.DeviceIdType.MESH
 F32 = jnp.float32
@@ -58,10 +58,20 @@
         cols = pl.ds(pl.multiple_of(k * CHUNK, CHUNK), CHUNK)
         return pltpu.make_async_copy(w_ref.at[:, cols], wv.at[k], w_sem.at[k])
 
+    acts_copies = []
+    for o in range(1, n_row):
+        to = lax.rem(r + o, n_row)
+        acts_copies.append(pltpu.make_async_remote_copy(
+            src_ref=hq.at[my_rows], dst_ref=hq.at[my_rows], send_sem=hr_sem.at[0, o - 1],
+            recv_sem=hr_sem.at[1, o - 1], device_id={"row": to}, device_id_type=MESH))
+
+    own_copy.wait()
     for k in range(EARLY):
         weight_copy(k).start()
-
-    own_copy.wait()
+    pl.semaphore_wait(barrier, peers - 1)
+    for copy in acts_copies:
+        copy.start()
+
     whole = depth // LANES
     for g in range(groups):
         at = pl.ds(pl.multiple_of(r * rows + g * LANES, LANES), LANES)
@@ -76,22 +86,12 @@
         pk[g:g + 1, :] = peak
         prec[me, g:g + 1, :] = peak
 
-    pl.semaphore_wait(barrier, peers - 1)
-
     def peak_copy(i, p, slot):
         return pltpu.make_async_remote_copy(
             src_ref=pk, dst_ref=prec.at[slot], send_sem=pk_send.at[i],
             recv_sem=pk_recv.at[slot], device_id=place(p), device_id_type=MESH)
 
     each_peer(lambda i, p: peak_copy(i, p, me).start())
-    acts_copies = []
-    for o in range(1, n_row):
-        to = lax.rem(r + o, n_row)
-        acts_copies.append(pltpu.make_async_remote_copy(
-            src_ref=hq.at[my_rows], dst_ref=hq.at[my_rows], send_sem=hr_sem.at[0, o - 1],
-            recv_sem=hr_sem.at[1, o - 1], device_id={"row": to}, device_id_type=MESH))
-    for copy in acts_copies:
-        copy.start()
     for k in range(EARLY, chunks):
         weight_copy(k).start()
 
@@ -134,7 +134,7 @@
     near_peer = 4 * far + 2 * (1 - near) + y
 
     def near_first(k):
-        return lax.rem(k, 4) == 1
+        return jnp.logical_and(k < 6, lax.rem(k, 2) == 1)
 
     def copy1(k):
         return pltpu.make_async_remote_copy(
@@ -195,12 +195,12 @@
         def at(lag, do):
             pl.when(jnp.logical_and(k >= lag, k < chunks + lag))(lambda: do(k - lag))
         at(0, multiply)
-        at(LAG, add1)
-        at(2 * LAG, add2)
-        at(3 * LAG, add3)
+        at(LAGS[0], add1)
+        at(LAGS[1], add2)
+        at(LAGS[2], add3)
         return carry
 
-    lax.fori_loop(0, chunks + 3 * LAG, step, 0)
+    lax.fori_loop(0, chunks + LAGS[2], step, 0)
 
     mrec[me] = mx[...]
 

time: 49.8 us -> 49.7 us (level)
  no operation moved by 1% of the time
where the time goes in v5:
time: 49.7 us; the launch traced here: 49.5 us
  Pallas kernels  48.9 us (98%)
  between operations  0.64 us (1%)
    pallas_call x1, Pallas kernels, on_device(): pl.pallas_call(functools.partial(kernel, n_row, n_col), out_shape=out_sha...  47.2 us
    pallas_call x1, Pallas kernels, on_device(): pl.pallas_call(write_out, out_shape=out_shape, in_specs=[vmem, vmem, smem...  1.7 us

profile of v5, /device:TPU:0, one launch (start us, length us, event | category | flops | bytes accessed | tf_op | source)
XLA Modules:
  0.0 49.5 jit_solution(5141938886486422562)
XLA Ops:
  0.6 47.2 %shard_map.58 = (bf16[32,4096]{1,0:T(8,128)(2,1)}, f32[1,128]{1,0:T(1,128)}, f32[4]{0:T(128)}) custom-call(bf16[128,3328]{1,0:T(8,128)(2,1)} %h_ref.1, bf16[3328,4096]{1,0:T(8,128)(2,1)} %w_ref.1, f32[4]{0:T(128)} %hist_ref.1), custom_call_target="tpu_custom_call" | custom-call | flops 6979321856 | bytes 27262976 | tf_op jit(solution)/shard_map/pallas_call | solution.py:255
  47.8 1.7 %shard_map.59 = (bf16[32,4096]{1,0:T(8,128)(2,1)}, f32[1,128]{1,0:T(1,128)}, f32[4]{0:T(128)}) custom-call(bf16[32,4096]{1,0:T(8,128)(2,1)} %get-tuple-element.9.a_ref, f32[1,128]{1,0:T(1,128)} %get-tuple-element.10.b_ref, f32[4]{0:T(128)} %get-tuple-element.11.c_ref), custom_call_target="tpu_custom_call" | custom-call | tf_op jit(solution)/shard_map/pallas_call | solution.py:285

commit v6 on v5

--- a/solution.py
+++ b/solution.py
@@ -12,7 +12,7 @@
 LANES = 128
 CHUNK = 256
 LAGS = (5, 8, 11)
-EARLY = 4
+WIDE = 4
 MESH = pl.DeviceIdType.MESH
 F32 = jnp.float32
 BF16 = jnp.bfloat16
@@ -27,7 +27,7 @@
 ):
     rows, depth = h_ref.shape
     groups = rows // LANES
-    chunks = wv.shape[0]
+    chunks = wv.shape[0] * WIDE
     n_far = n_col // 4
     half = rows * n_row // 2
     quarter = half // 2
@@ -55,7 +55,7 @@
     own_copy.start()
 
     def weight_copy(k):
-        cols = pl.ds(pl.multiple_of(k * CHUNK, CHUNK), CHUNK)
+        cols = pl.ds(pl.multiple_of(k * WIDE * CHUNK, CHUNK), WIDE * CHUNK)
         return pltpu.make_async_copy(w_ref.at[:, cols], wv.at[k], w_sem.at[k])
 
     acts_copies = []
@@ -66,8 +66,7 @@
             recv_sem=hr_sem.at[1, o - 1], device_id={"row": to}, device_id_type=MESH))
 
     own_copy.wait()
-    for k in range(EARLY):
-        weight_copy(k).start()
+    weight_copy(0).start()
     pl.semaphore_wait(barrier, peers - 1)
     for copy in acts_copies:
         copy.start()
@@ -92,7 +91,7 @@
             recv_sem=pk_recv.at[slot], device_id=place(p), device_id_type=MESH)
 
     each_peer(lambda i, p: peak_copy(i, p, me).start())
-    for k in range(EARLY, chunks):
+    for k in range(1, chunks // WIDE):
         weight_copy(k).start()
 
     each_peer(lambda i, p: peak_copy(i, p, p).wait_recv())
@@ -134,7 +133,7 @@
     near_peer = 4 * far + 2 * (1 - near) + y
 
     def near_first(k):
-        return jnp.logical_and(k < 6, lax.rem(k, 2) == 1)
+        return lax.rem(k, 4) == 1
 
     def copy1(k):
         return pltpu.make_async_remote_copy(
@@ -156,8 +155,9 @@
             device_id={"col": to}, device_id_type=MESH)
 
     def multiply(k):
-        weight_copy(k).wait()
-        p = jnp.dot(xq[...], wv[k], preferred_element_type=F32)
+        pl.when(lax.rem(k, WIDE) == 0)(lambda: weight_copy(k // WIDE).wait())
+        cols = pl.ds(pl.multiple_of(lax.rem(k, WIDE) * CHUNK, CHUNK), CHUNK)
+        p = jnp.dot(xq[...], wv[k // WIDE, :, cols], preferred_element_type=F32)
         p1, p2 = p[quarter:half], p[half:half + quarter]
         swap = near_first(k)
         send1[k, :quarter] = p[:quarter].astype(BF16)
@@ -261,7 +261,7 @@
             pltpu.VMEM((tokens, depth), BF16),
             pltpu.VMEM((tokens, depth), BF16),
             pltpu.VMEM((tokens, LANES), BF16),
-            pltpu.VMEM((chunks, depth, CHUNK), BF16),
+            pltpu.VMEM((chunks // WIDE, depth, WIDE * CHUNK), BF16),
             pltpu.VMEM((groups, LANES), F32),
             pltpu.VMEM((peers, groups, LANES), F32),
             pltpu.VMEM((chunks, half, CHUNK), BF16),
@@ -273,7 +273,7 @@
             pltpu.VMEM((chunks, n_far - 1, block, CHUNK), BF16),
             pltpu.VMEM((1, LANES), F32),
             pltpu.VMEM((peers, 1, LANES), F32),
-            dma, dma((2, n_row - 1)), dma((chunks,)), dma((peers,)), dma((peers,)),
+            dma, dma((2, n_row - 1)), dma((chunks // WIDE,)), dma((peers,)), dma((peers,)),
             dma((2, chunks)), dma((2, chunks)), dma((chunks, n_far - 1)), dma((chunks, n_far - 1)),
             dma((peers,)), dma((peers,)),
         ],

time: 49.7 us -> 49.3 us (level)
  no operation moved by 1% of the time
where the time goes in v6:
time: 49.3 us; the launch traced here: 49.1 us
  Pallas kernels  48.5 us (98%)
  between operations  0.64 us (1%)
    pallas_call x1, Pallas kernels, on_device(): pl.pallas_call(functools.partial(kernel, n_row, n_col), out_shape=out_sha...  46.8 us
    pallas_call x1, Pallas kernels, on_device(): pl.pallas_call(write_out, out_shape=out_shape, in_specs=[vmem, vmem, smem...  1.7 us

profile of v6, /device:TPU:0, one launch (start us, length us, event | category | flops | bytes accessed | tf_op | source)
XLA Modules:
  0.0 49.1 jit_solution(2539078470349471637)
XLA Ops:
  0.6 46.8 %shard_map.58 = (bf16[32,4096]{1,0:T(8,128)(2,1)}, f32[1,128]{1,0:T(1,128)}, f32[4]{0:T(128)}) custom-call(bf16[128,3328]{1,0:T(8,128)(2,1)} %h_ref.1, bf16[3328,4096]{1,0:T(8,128)(2,1)} %w_ref.1, f32[4]{0:T(128)} %hist_ref.1), custom_call_target="tpu_custom_call" | custom-call | flops 6979321856 | bytes 27262976 | tf_op jit(solution)/shard_map/pallas_call | solution.py:255
  47.4 1.7 %shard_map.59 = (bf16[32,4096]{1,0:T(8,128)(2,1)}, f32[1,128]{1,0:T(1,128)}, f32[4]{0:T(128)}) custom-call(bf16[32,4096]{1,0:T(8,128)(2,1)} %get-tuple-element.9.a_ref, f32[1,128]{1,0:T(1,128)} %get-tuple-element.10.b_ref, f32[4]{0:T(128)} %get-tuple-element.11.c_ref), custom_call_target="tpu_custom_call" | custom-call | tf_op jit(solution)/shard_map/pallas_call | solution.py:285
